TPU v7x, 32 devices: a whole 2x2x4 slice. The times are simulated.
32 devices in a mesh: chan: 16 (over z, x, core), rows: 2 (over y).
Axes of the slice: x: 2, y: 2, z: 4, core: 2. Of those that a mesh axis runs over, the one named last changes fastest.
Arguments:
- inputs: bfloat16 [1, 2, 256, 2048], P(None, 'rows', None, 'chan'), may hold values from -6 to 6
- weights: bfloat16 [3, 3, 2048, 2048], P(None, None, 'chan'), may hold values from -0.0625 to 0.0625
- cotangent: bfloat16 [1, 2, 256, 2048], P(None, 'rows', None, 'chan'), may hold values from -6 to 6
Outputs:
- outputs: bfloat16 [1, 2, 256, 2048], P(None, 'rows', None, 'chan')
- input_grad: bfloat16 [1, 2, 256, 2048], P(None, 'rows', None, 'chan')
- weight_grad: float32 [3, 3, 2048, 2048], P(None, None, 'chan', 'rows')
All inputs are finite; a program needn't handle non-finite values.
Results may differ from a plain program's by a relative error of at most 0.001.
Values may be sent and summed in bfloat16 or wider, within the bound.
A program may use at most 128 MiB of HBM per device.

v0:
```python
import jax
import jax.numpy as jnp
from jax import lax
from jax.sharding import PartitionSpec as P


def taps_of(padded, height, breadth):
    return [
        padded[:, ky : ky + height, kx : kx + breadth, :].reshape(-1, padded.shape[3])
        for ky in range(3)
        for kx in range(3)
    ]


def rim(array):
    return jnp.pad(array, ((0, 0), (1, 1), (1, 1), (0, 0)))


def on_device(inputs, weights, cotangent):
    batches, height, breadth, local_ch = inputs.shape
    channels = weights.shape[3]
    groups = lax.axis_size("rows")
    row = lax.axis_index("rows")
    share = channels // groups
    total_pixels = batches * height * groups * breadth

    def around(padded):
        return lax.dynamic_slice_in_dim(padded, row * height, height + 2, axis=1)

    in_padded = rim(lax.all_gather(inputs, "rows", axis=1, tiled=True))
    cot_all = lax.all_gather(
        lax.all_gather(cotangent, "chan", axis=3, tiled=True), "rows", axis=1, tiled=True
    )
    columns = jnp.concatenate(taps_of(around(in_padded), height, breadth), axis=1)
    conv_out = lax.psum_scatter(
        lax.dot_general(
            weights.reshape(9 * local_ch, channels),
            columns,
            (((0,), (1,)), ((), ())),
            preferred_element_type=jnp.float32,
        ),
        "chan",
        scatter_dimension=0,
        tiled=True,
    )
    outputs = conv_out.T.reshape(batches, height, breadth, local_ch).astype(jnp.bfloat16)
    grad_taps = taps_of(around(rim(cot_all)), height, breadth)
    data_sum = 0.0
    for tap in range(9):
        data_sum += lax.dot_general(
            grad_taps[8 - tap],
            weights[tap // 3, tap % 3],
            (((1,), (1,)), ((), ())),
            preferred_element_type=jnp.float32,
        )
    input_grad = data_sum.reshape(batches, height, breadth, local_ch).astype(jnp.bfloat16)
    all_columns = jnp.concatenate(taps_of(in_padded, height * groups, breadth), axis=1)
    mine = lax.dynamic_slice_in_dim(cot_all, row * share, share, axis=3)
    update = lax.dot_general(
        all_columns,
        mine.reshape(total_pixels, share),
        (((0,), (0,)), ((), ())),
        preferred_element_type=jnp.float32,
    )
    weight_grad = (update / jnp.sqrt(jnp.float32(total_pixels))).reshape(3, 3, local_ch, share)
    return (outputs, input_grad, weight_grad)


def solution(mesh):
    in_specs = (
        P(None, "rows", None, "chan"),
        P(None, None, "chan", None),
        P(None, "rows", None, "chan"),
    )
    out_specs = (
        P(None, "rows", None, "chan"),
        P(None, "rows", None, "chan"),
        P(None, None, "chan", "rows"),
    )
    return jax.shard_map(
        on_device, mesh=mesh, in_specs=in_specs, out_specs=out_specs, check_vma=False
    )
```

profile of v0, /device:TPU:0, one launch (start us, length us, event | category | flops | bytes accessed | tf_op | source)
XLA Modules:
  0.0 166.6 jit_solution(7292825136925069916)
XLA Ops:
  7.2 0.0 all-gather.3.cloned.1.call-start
  7.2 0.7 all-gather.3.cloned.1.call-update
  7.9 0.0 reduce-scatter.2.cloned.1.call-start
  7.9 6.1 %all_gather.9 = bf16[1,2,256,128]{3,2,0,1:T(8,128)(2,1)S(1)} all-gather(bf16[1,1,256,128]{3,2,0,1:T(8,128)(2,1)} %bitcast.139), channel_id=1, replica_groups=mesh['chan'=16,'rows'=2] {'rows'}, dimensions={1}, use_global_device_ids=true | all-gather | bytes 196608 | tf_op jit(solution)/shard_map/all_gather | solution.py:30
  14.1 0.1 fusion.39
  14.4 0.1 fusion.41
  14.5 5.2 %convolution_bitcast_fusion = f32[2048,256]{0,1:T(8,128)} fusion(bf16[256,1152]{1,0:T(8,128)(2,1)S(1)} %fusion.41, bf16[1152,2048]{1,0:T(8,128)(2,1)} %bitcast.126), kind=kOutput, calls=%fused_computation.10 | convolution fusion | flops 1207959552 | bytes 7405568 | tf_op jit(solution)/shard_map/dot_general | solution.py:36
  19.7 0.0 all-gather.5.cloned.1.call-start
  19.8 29.9 %all-gather.3.cloned.1.call-done = bf16[1,1,256,2048]{3,2,0,1:T(8,128)(2,1)} async-done(((bf16[1,1,256,128]{3,2,0,1:T(8,128)(2,1)}), bf16[1,1,256,2048]{3,2,0,1:T(8,128)(2,1)}) %all-gather.3.cloned.1.call-update) | async-done | bytes 1048592 | tf_op jit(solution)/shard_map/all_gather | solution.py:32
  49.7 0.1 pad_slice_fusion
  50.2 64.8 %reduce-scatter.2.cloned.1.call-done = f32[128,256]{0,1:T(8,128)} async-done(((f32[2048,256]{0,1:T(8,128)}), f32[128,256]{0,1:T(8,128)}) %reduce-scatter.2.cloned.1.call-update) | async-done | bytes 131088 | tf_op jit(solution)/shard_map/reduce_scatter | solution.py:35
  115.0 1.5 convert_bitcast_fusion
  116.6 32.3 %all-gather.5.cloned.1.call-done = bf16[1,2,256,2048]{3,2,0,1:T(8,128)(2,1)} async-done(((bf16[1,1,256,2048]{3,2,0,1:T(8,128)(2,1)}), bf16[1,2,256,2048]{3,2,0,1:T(8,128)(2,1)}) %all-gather.5.cloned.1.call-update) | async-done | bytes 2097168 | tf_op jit(solution)/shard_map/all_gather | solution.py:31
  148.9 1.4 constant_dynamic-slice_fusion
  150.3 3.6 %convolution_multiply_fusion = f32[1152,1024]{1,0:T(8,128)} fusion(bf16[512,1152]{1,0:T(8,128)(2,1)S(1)} %constant_dynamic-update-slice_fusion, bf16[512,1024]{1,0:T(8,128)(2,1)S(1)} %bitcast.129), kind=kOutput, calls=%fused_computation.9 | convolution fusion | flops 1209139200 | bytes 6946816 | tf_op jit(solution)/shard_map/dot_general | solution.py:59
  154.0 1.5 fusion.19
  155.5 0.5 convolution_add_fusion.7
  156.0 0.5 convolution_add_fusion.6
  156.5 0.5 convolution_add_fusion.5
  157.0 0.4 convolution_add_fusion.4
  157.5 0.5 convolution_add_fusion.3
  158.0 0.5 convolution_add_fusion.2
  158.5 0.4 convolution_add_fusion.1
  158.9 1.1 fusion.1
  (26 shorter events, 0.6 us)
Async XLA Ops:
  7.2 42.5 %all-gather.3.cloned.1.call-start = ((), (), s32[]{:S(2)}) async-start(), calls=%async_computation.2 | async-start | bytes 1114112 | tf_op jit(solution)/shard_map/all_gather | solution.py:32
  7.9 107.1 %reduce-scatter.2.cloned.1.call-start = ((), (), s32[]{:S(2)}) async-start(), calls=%async_computation.1 | async-start | bytes 2228224 | tf_op jit(solution)/shard_map/reduce_scatter | solution.py:35
  19.7 129.1 %all-gather.5.cloned.1.call-start = ((), (), s32[]{:S(2)}) async-start(), calls=%async_computation.3 | async-start | bytes 3145728 | tf_op jit(solution)/shard_map/all_gather | solution.py:31
  148.9 6.6 %slice-start = ((s8[4718592]{0:T(1024)(128)(4,1)}), s8[4194304]{0:T(1024)(128)(4,1)S(1)}, s32[]{:S(2)}) async-start(s8[4718592]{0:T(1024)(128)(4,1)} %bitcast.127), calls=%async_computation.4 | async-start | bytes 8388608
  150.3 3.7 %copy-start = (bf16[1,2,256,2048]{3,2,0,1:T(8,128)(2,1)S(1)}, bf16[1,2,256,2048]{3,2,0,1:T(8,128)(2,1)}, u32[]{:S(2)}) copy-start(bf16[1,2,256,2048]{3,2,0,1:T(8,128)(2,1)} %all-gather.5.cloned.1.call-done) | copy-start | bytes 6291460
  150.3 5.2 %slice-start.1 = ((s8[4718592]{0:T(1024)(128)(4,1)}), s8[524288]{0:T(1024)(128)(4,1)S(1)}, s32[]{:S(2)}) async-start(s8[4718592]{0:T(1024)(128)(4,1)} %bitcast.127), calls=%async_computation.5 | async-start | bytes 1048576
Sparse Core Ops, SparseCore 0:
  10.2 39.4 all-gather.2
  54.0 60.9 reduce-scatter.1
  116.7 32.1 all-gather.4
where the time goes:
time: 167 us
  waiting for transfers between devices  128 us (77%)
  matrix products  14.9 us (9%)
  between operations  14 us (8%)
  blocking collectives  6.14 us (4%)
  local copies, waits for them, and re-layouts  2.23 us (1%)
    reduce_scatter x1, waiting for transfers between devices, on_device(): lax.psum_scatter(lax.dot_general(weights.reshape(9 * local_ch, channels),...  64.8 us
    all_gather x1, waiting for transfers between devices, on_device(): lax.all_gather(lax.all_gather(cotangent, 'chan', axis=3, tiled=True), 'ro...  32.3 us
    all_gather x1, waiting for transfers between devices, on_device(): lax.all_gather(cotangent, 'chan', axis=3, tiled=True)  29.9 us
    all_gather x1, blocking collectives, on_device(): in_padded = rim(lax.all_gather(inputs, 'rows', axis=1, tiled=True))  6.14 us
    dot_general x9, matrix products, on_device(): lax.dot_general(grad_taps[8 - tap], weights[tap // 3, tap % 3], (((1,), (...  6.04 us
    dot_general x1, matrix products, on_device(): lax.dot_general(weights.reshape(9 * local_ch, channels), columns, (((0,),...  5.23 us
    dot_general x1, matrix products, on_device(): lax.dot_general(all_columns, mine.reshape(total_pixels, share), (((0,), (...  3.62 us
  transfers between devices with their start and end apart: 3, of which 3 were waited for; matrix products, arithmetic and copies ran while one was open for 5% of the time, Pallas kernels for 0%

commit v1 on v0

--- a/solution.py
+++ b/solution.py
@@ -2,6 +2,32 @@
 import jax.numpy as jnp
 from jax import lax
 from jax.sharding import PartitionSpec as P
+
+
+def figure_set(original, axis_k):
+    earlier = list(original.shape[1:])
+    earlier[axis_k] *= original.shape[0]
+    z_new = jnp.moveaxis(original, 0, axis_k).reshape(earlier)
+    return z_new
+
+
+def _get_types(mat, group_axis, d_out):
+    num = lax.axis_size(group_axis)
+    trail = [(pp, (pp + 1) % num) for pp in range(num)]
+    outcome_arr, aux = ([], [])
+    row_list = [(k0, k) for k, k0 in trail]
+    for u in range(num - 1):
+        if u % 2 == 0:
+            outcome_arr.append(
+                lax.ppermute(outcome_arr[-1] if outcome_arr else mat, group_axis, trail)
+            )
+        else:
+            aux.append(lax.ppermute(aux[-1] if aux else mat, group_axis, row_list))
+    finding = jnp.stack([*outcome_arr[::-1], mat, *aux])
+    block_next = lax.axis_index(group_axis) - len(outcome_arr)
+    finding = finding[(jnp.arange(num) - block_next) % num]
+    block_last = figure_set(finding, d_out)
+    return block_last
 
 
 def taps_of(padded, height, breadth):
@@ -28,9 +54,7 @@
         return lax.dynamic_slice_in_dim(padded, row * height, height + 2, axis=1)
 
     in_padded = rim(lax.all_gather(inputs, "rows", axis=1, tiled=True))
-    cot_all = lax.all_gather(
-        lax.all_gather(cotangent, "chan", axis=3, tiled=True), "rows", axis=1, tiled=True
-    )
+    cot_all = lax.all_gather(_get_types(cotangent, "chan", 3), "rows", axis=1, tiled=True)
     columns = jnp.concatenate(taps_of(around(in_padded), height, breadth), axis=1)
     conv_out = lax.psum_scatter(
         lax.dot_general(

time: 167 us -> 145 us (0.87)
  waiting for transfers between devices: 128 us -> 68 us
  starting transfers between devices: 0.12 us -> 30.9 us
  local copies, waits for them, and re-layouts: 2.23 us -> 6.45 us
  matrix products: 14.9 us -> 17.1 us
  between operations: 14 us -> 15.8 us
    reduce_scatter x1, waiting for transfers between devices: 64.8 us -> 20 us  [on_device(): lax.psum_scatter(lax.dot_general(weights.reshape(9 * local_ch, channels),...]
    all_gather x2 -> x1, waiting for transfers between devices: 62.2 us -> 28.6 us  [on_device(): lax.all_gather(_get_types(cotangent, 'chan', 3), 'rows', axis=1, tiled=True)]
    ppermute x0 -> x15, starting transfers between devices: none -> 30.8 us  [the longest x7 30.3 us: _get_types(): aux.append(lax.ppermute(aux[-1] if aux else mat, group_axis, row_list))]
    ppermute x0 -> x15, waiting for transfers between devices: none -> 19.4 us  [the longest x8 10.8 us: _get_types(): lax.ppermute(outcome_arr[-1] if outcome_arr else mat, group_axis, trail)]
    dot_general x9, matrix products: 6.04 us -> 8.25 us  [on_device(): lax.dot_general(grad_taps[8 - tap], weights[tap // 3, tap % 3], (((1,), (...]
  transfers between devices with their start and end apart: 3 -> 17, of which waited for: 3 -> 11; matrix products, arithmetic and copies ran while one was open for 5% -> 14% of each run, Pallas kernels for 0% -> 0%
where the time goes in v1:
time: 145 us
  waiting for transfers between devices  68 us (47%)
  starting transfers between devices  30.9 us (21%)
  matrix products  17.1 us (12%)
  between operations  15.8 us (11%)
  local copies, waits for them, and re-layouts  6.45 us (4%)
  blocking collectives  5.19 us (4%)
  other arithmetic  1.56 us (1%)
    ppermute x7, starting transfers between devices, _get_types(): aux.append(lax.ppermute(aux[-1] if aux else mat, group_axis, row_list))  30.3 us
    all_gather x1, waiting for transfers between devices, on_device(): lax.all_gather(_get_types(cotangent, 'chan', 3), 'rows', axis=1, tiled=True)  28.6 us
    reduce_scatter x1, waiting for transfers between devices, on_device(): lax.psum_scatter(lax.dot_general(weights.reshape(9 * local_ch, channels),...  20 us
    ppermute x8, waiting for transfers between devices, _get_types(): lax.ppermute(outcome_arr[-1] if outcome_arr else mat, group_axis, trail)  10.8 us
    ppermute x7, waiting for transfers between devices, _get_types(): aux.append(lax.ppermute(aux[-1] if aux else mat, group_axis, row_list))  8.55 us
    dot_general x9, matrix products, on_device(): lax.dot_general(grad_taps[8 - tap], weights[tap // 3, tap % 3], (((1,), (...  8.25 us
    dot_general x1, matrix products, on_device(): lax.dot_general(weights.reshape(9 * local_ch, channels), columns, (((0,),...  5.22 us
    all_gather x1, blocking collectives, on_device(): in_padded = rim(lax.all_gather(inputs, 'rows', axis=1, tiled=True))  5.19 us
  transfers between devices with their start and end apart: 17, of which 11 were waited for; matrix products, arithmetic and copies ran while one was open for 14% of the time, Pallas kernels for 0%

profile of v1, /device:TPU:0, one launch (start us, length us, event | category | flops | bytes accessed | tf_op | source)
XLA Modules:
  0.0 145.0 jit_solution(15707414051056075180)
XLA Ops:
  8.5 7.1 %collective-permute-done = bf16[1,1,256,128]{3,2,1,0:T(8,128)(2,1)S(1)} collective-permute-done((bf16[1,1,256,128]{3,2,1,0:T(8,128)(2,1)}, bf16[1,1,256,128]{3,2,1,0:T(8,128)(2,1)S(1)}, u32[]{:S(2)}, u32[]{:S(2)}) %collective-permute-start) | collective-permute-done | bytes 65568 | tf_op jit(solution)/shard_map/ppermute | solution.py:22
  15.7 4.4 %collective-permute-start.8 = (bf16[1,1,256,128]{3,2,1,0:T(8,128)(2,1)}, bf16[1,1,256,128]{3,2,1,0:T(8,128)(2,1)S(1)}, u32[]{:S(2)}, u32[]{:S(2)}) collective-permute-start(bf16[1,1,256,128]{3,2,1,0:T(8,128)(2,1)} %param.5), channel_id=1, source_target_pairs={{2,0},{4,2},{6,4},{8,6},{10,8},{12,10},{14,12},{16,14},{18,16},{20... | collective-permute-start | bytes 196616 | tf_op jit(solution)/shard_map/ppermute | solution.py:25
  20.1 1.9 %collective-permute-done.1 = bf16[1,1,256,128]{3,2,1,0:T(8,128)(2,1)S(1)} collective-permute-done((bf16[1,1,256,128]{3,2,1,0:T(8,128)(2,1)S(1)}, bf16[1,1,256,128]{3,2,1,0:T(8,128)(2,1)S(1)}, u32[]{:S(2)}, u32[]{:S(2)}) %collective-permute-start.1) | collective-permute-done | bytes 65568 | tf_op jit(solution)/shard_map/ppermute | solution.py:22
  22.3 4.4 %collective-permute-start.9 = (bf16[1,1,256,128]{3,2,1,0:T(8,128)(2,1)S(1)}, bf16[1,1,256,128]{3,2,1,0:T(8,128)(2,1)S(1)}, u32[]{:S(2)}, u32[]{:S(2)}) collective-permute-start(bf16[1,1,256,128]{3,2,1,0:T(8,128)(2,1)S(1)} %collective-permute-done.8), channel_id=1, source_target_pairs={{2,0},{4,2},{6,4},{8,6},{10,8},{12,10},{14,12},{16,14},{18,16},{20... | collective-permute-start | bytes 196616 | tf_op jit(solution)/shard_map/ppermute | solution.py:25
  26.7 1.7 %collective-permute-done.2 = bf16[1,1,256,128]{3,2,1,0:T(8,128)(2,1)S(1)} collective-permute-done((bf16[1,1,256,128]{3,2,1,0:T(8,128)(2,1)S(1)}, bf16[1,1,256,128]{3,2,1,0:T(8,128)(2,1)S(1)}, u32[]{:S(2)}, u32[]{:S(2)}) %collective-permute-start.2) | collective-permute-done | bytes 65568 | tf_op jit(solution)/shard_map/ppermute | solution.py:22
  28.5 5.2 %all_gather.6 = bf16[1,2,256,128]{3,2,0,1:T(8,128)(2,1)S(1)} all-gather(bf16[1,1,256,128]{3,2,0,1:T(8,128)(2,1)} %bitcast.208), channel_id=1, replica_groups=mesh['chan'=16,'rows'=2] {'rows'}, dimensions={1}, use_global_device_ids=true | all-gather | bytes 196608 | tf_op jit(solution)/shard_map/all_gather | solution.py:56
  33.6 3.6 %collective-permute-start.10 = (bf16[1,1,256,128]{3,2,1,0:T(8,128)(2,1)S(1)}, bf16[1,1,256,128]{3,2,1,0:T(8,128)(2,1)S(1)}, u32[]{:S(2)}, u32[]{:S(2)}) collective-permute-start(bf16[1,1,256,128]{3,2,1,0:T(8,128)(2,1)S(1)} %collective-permute-done.9), channel_id=1, source_target_pairs={{2,0},{4,2},{6,4},{8,6},{10,8},{12,10},{14,12},{16,14},{18,16},{20... | collective-permute-start | bytes 196616 | tf_op jit(solution)/shard_map/ppermute | solution.py:25
  37.3 1.8 %collective-permute-done.10 = bf16[1,1,256,128]{3,2,1,0:T(8,128)(2,1)S(1)} collective-permute-done((bf16[1,1,256,128]{3,2,1,0:T(8,128)(2,1)S(1)}, bf16[1,1,256,128]{3,2,1,0:T(8,128)(2,1)S(1)}, u32[]{:S(2)}, u32[]{:S(2)}) %collective-permute-start.10) | collective-permute-done | bytes 65568 | tf_op jit(solution)/shard_map/ppermute | solution.py:25
  39.1 4.5 %collective-permute-start.11 = (bf16[1,1,256,128]{3,2,1,0:T(8,128)(2,1)S(1)}, bf16[1,1,256,128]{3,2,1,0:T(8,128)(2,1)S(1)}, u32[]{:S(2)}, u32[]{:S(2)}) collective-permute-start(bf16[1,1,256,128]{3,2,1,0:T(8,128)(2,1)S(1)} %collective-permute-done.10), channel_id=1, source_target_pairs={{2,0},{4,2},{6,4},{8,6},{10,8},{12,10},{14,12},{16,14},{18,16},{20... | collective-permute-start | bytes 196616 | tf_op jit(solution)/shard_map/ppermute | solution.py:25
  43.6 1.9 %collective-permute-done.11 = bf16[1,1,256,128]{3,2,1,0:T(8,128)(2,1)S(1)} collective-permute-done((bf16[1,1,256,128]{3,2,1,0:T(8,128)(2,1)S(1)}, bf16[1,1,256,128]{3,2,1,0:T(8,128)(2,1)S(1)}, u32[]{:S(2)}, u32[]{:S(2)}) %collective-permute-start.11) | collective-permute-done | bytes 65568 | tf_op jit(solution)/shard_map/ppermute | solution.py:25
  45.5 4.5 %collective-permute-start.12 = (bf16[1,1,256,128]{3,2,1,0:T(8,128)(2,1)S(1)}, bf16[1,1,256,128]{3,2,1,0:T(8,128)(2,1)S(1)}, u32[]{:S(2)}, u32[]{:S(2)}) collective-permute-start(bf16[1,1,256,128]{3,2,1,0:T(8,128)(2,1)S(1)} %collective-permute-done.11), channel_id=1, source_target_pairs={{2,0},{4,2},{6,4},{8,6},{10,8},{12,10},{14,12},{16,14},{18,16},{20... | collective-permute-start | bytes 196616 | tf_op jit(solution)/shard_map/ppermute | solution.py:25
  50.0 1.9 %collective-permute-done.12 = bf16[1,1,256,128]{3,2,1,0:T(8,128)(2,1)S(1)} collective-permute-done((bf16[1,1,256,128]{3,2,1,0:T(8,128)(2,1)S(1)}, bf16[1,1,256,128]{3,2,1,0:T(8,128)(2,1)S(1)}, u32[]{:S(2)}, u32[]{:S(2)}) %collective-permute-start.12) | collective-permute-done | bytes 65568 | tf_op jit(solution)/shard_map/ppermute | solution.py:25
  51.9 4.5 %collective-permute-start.13 = (bf16[1,1,256,128]{3,2,1,0:T(8,128)(2,1)S(1)}, bf16[1,1,256,128]{3,2,1,0:T(8,128)(2,1)S(1)}, u32[]{:S(2)}, u32[]{:S(2)}) collective-permute-start(bf16[1,1,256,128]{3,2,1,0:T(8,128)(2,1)S(1)} %collective-permute-done.12), channel_id=1, source_target_pairs={{2,0},{4,2},{6,4},{8,6},{10,8},{12,10},{14,12},{16,14},{18,16},{20... | collective-permute-start | bytes 196616 | tf_op jit(solution)/shard_map/ppermute | solution.py:25
  56.4 1.9 %collective-permute-done.13 = bf16[1,1,256,128]{3,2,1,0:T(8,128)(2,1)S(1)} collective-permute-done((bf16[1,1,256,128]{3,2,1,0:T(8,128)(2,1)S(1)}, bf16[1,1,256,128]{3,2,1,0:T(8,128)(2,1)S(1)}, u32[]{:S(2)}, u32[]{:S(2)}) %collective-permute-start.13) | collective-permute-done | bytes 65568 | tf_op jit(solution)/shard_map/ppermute | solution.py:25
  58.3 4.5 %collective-permute-start.14 = (bf16[1,1,256,128]{3,2,1,0:T(8,128)(2,1)S(1)}, bf16[1,1,256,128]{3,2,1,0:T(8,128)(2,1)S(1)}, u32[]{:S(2)}, u32[]{:S(2)}) collective-permute-start(bf16[1,1,256,128]{3,2,1,0:T(8,128)(2,1)S(1)} %collective-permute-done.13), channel_id=1, source_target_pairs={{2,0},{4,2},{6,4},{8,6},{10,8},{12,10},{14,12},{16,14},{18,16},{20... | collective-permute-start | bytes 196616 | tf_op jit(solution)/shard_map/ppermute | solution.py:25
  67.8 5.2 %convolution_bitcast_fusion = f32[2048,256]{0,1:T(8,128)} fusion(bf16[256,1152]{1,0:T(8,128)(2,1)S(1)} %constant_dynamic-update-slice_fusion, bf16[1152,2048]{1,0:T(8,128)(2,1)} %bitcast.192), kind=kOutput, calls=%fused_computation.11 | convolution fusion | flops 1207959552 | bytes 7405568 | tf_op jit(solution)/shard_map/dot_general | solution.py:60
  73.6 28.6 %all-gather.2.cloned.1.call-done = bf16[1,2,256,2048]{3,2,0,1:T(8,128)(2,1)} async-done(((bf16[1,1,256,2048]{3,2,0,1:T(8,128)(2,1)}), bf16[1,2,256,2048]{3,2,0,1:T(8,128)(2,1)}) %all-gather.2.cloned.1.call-update) | async-done | bytes 2097168 | tf_op jit(solution)/shard_map/all_gather | solution.py:57
  102.2 1.4 constant_dynamic-slice_fusion
  104.1 1.7 %fusion.19 = f32[256,128]{1,0:T(8,128)S(1)} fusion(s32[]{:T(128)S(6)} %add.73, s32[]{:T(128)S(6)} %add.74, bf16[1,2,256,2048]{3,2,0,1:T(8,128)(2,1)S(1)} %copy-done, bf16[3,3,128,2048]{3,2,1,0:T(8,128)(2,1)} %param.4), kind=kOutput, calls=%fused_computation.31 | convolution fusion | flops 134217728 | bytes 2752520 | tf_op jit(solution)/shard_map/dot_general | solution.py:74
  105.8 1.5 %convolution_add_fusion.7 = f32[256,128]{1,0:T(8,128)S(1)} fusion(f32[256,128]{1,0:T(8,128)S(1)} %fusion.19, s32[]{:T(128)S(6)} %add.73, s32[]{:T(128)S(6)} %add.78, bf16[1,2,256,2048]{3,2,0,1:T(8,128)(2,1)S(1)} %copy-done, bf16[3,3,128,2048]{3,2,1,0:T(8,128)(2,1)} %param.4), kind=kOutput, calls=%fused_computation.19 | convolution fusion | flops 134250496 | bytes 2883592 | tf_op jit(solution)/shard_map/dot_general | solution.py:74
  107.3 1.5 %convolution_add_fusion.6 = f32[256,128]{1,0:T(8,128)S(1)} fusion(f32[256,128]{1,0:T(8,128)S(1)} %convolution_add_fusion.7, s32[]{:T(128)S(6)} %add.73, bf16[1,2,256,2048]{3,2,0,1:T(8,128)(2,1)S(1)} %copy-done, bf16[3,3,128,2048]{3,2,1,0:T(8,128)(2,1)} %param.4), kind=kOutput, calls=%fused_computation.18 | convolution fusion | flops 134250496 | bytes 2883588 | tf_op jit(solution)/shard_map/dot_general | solution.py:74
  112.4 3.6 %convolution_multiply_fusion = f32[1152,1024]{1,0:T(8,128)} fusion(bf16[512,1152]{1,0:T(8,128)(2,1)S(1)} %constant_dynamic-update-slice_fusion.25, bf16[512,1024]{1,0:T(8,128)(2,1)S(1)} %bitcast.197), kind=kOutput, calls=%fused_computation.10 | convolution fusion | flops 1209139200 | bytes 6946816 | tf_op jit(solution)/shard_map/dot_general | solution.py:83
  116.0 20.0 %reduce-scatter.2.cloned.1.call-done = f32[128,256]{0,1:T(8,128)} async-done(((f32[2048,256]{0,1:T(8,128)}), f32[128,256]{0,1:T(8,128)}) %reduce-scatter.2.cloned.1.call-update) | async-done | bytes 131088 | tf_op jit(solution)/shard_map/reduce_scatter | solution.py:59
  136.1 1.5 %convert_bitcast_fusion = bf16[1,1,256,128]{3,2,1,0:T(8,128)(2,1)} fusion(f32[128,256]{0,1:T(8,128)} %reduce-scatter.2.cloned.1.call-done), kind=kLoop, calls=%fused_computation.104 | loop fusion | flops 32768 | bytes 196608 | tf_op jit(solution)/shard_map/convert_element_type | solution.py:70
  (74 shorter events, 10.3 us)
Async XLA Ops:
  8.0 94.2 %all-gather.2.cloned.1.call-start = ((), (), s32[]{:S(2)}) async-start(), calls=%async_computation.2 | async-start | bytes 3145728 | tf_op jit(solution)/shard_map/all_gather | solution.py:57
  8.0 7.6 %collective-permute-start = (bf16[1,1,256,128]{3,2,1,0:T(8,128)(2,1)}, bf16[1,1,256,128]{3,2,1,0:T(8,128)(2,1)S(1)}, u32[]{:S(2)}, u32[]{:S(2)}) collective-permute-start(bf16[1,1,256,128]{3,2,1,0:T(8,128)(2,1)} %param.5), channel_id=1, source_target_pairs={{0,2},{2,4},{4,6},{6,8},{8,10},{10,12},{12,14},{14,16},{16,18},{18... | collective-permute-start | bytes 196616 | tf_op jit(solution)/shard_map/ppermute | solution.py:22
  15.7 6.4 %collective-permute-start.1 = (bf16[1,1,256,128]{3,2,1,0:T(8,128)(2,1)S(1)}, bf16[1,1,256,128]{3,2,1,0:T(8,128)(2,1)S(1)}, u32[]{:S(2)}, u32[]{:S(2)}) collective-permute-start(bf16[1,1,256,128]{3,2,1,0:T(8,128)(2,1)S(1)} %collective-permute-done), channel_id=1, source_target_pairs={{0,2},{2,4},{4,6},{6,8},{8,10},{10,12},{12,14},{14,16},{16,18},{18... | collective-permute-start | bytes 196616 | tf_op jit(solution)/shard_map/ppermute | solution.py:22
  15.7 6.7 %collective-permute-start.8 = (bf16[1,1,256,128]{3,2,1,0:T(8,128)(2,1)}, bf16[1,1,256,128]{3,2,1,0:T(8,128)(2,1)S(1)}, u32[]{:S(2)}, u32[]{:S(2)}) collective-permute-start(bf16[1,1,256,128]{3,2,1,0:T(8,128)(2,1)} %param.5), channel_id=1, source_target_pairs={{2,0},{4,2},{6,4},{8,6},{10,8},{12,10},{14,12},{16,14},{18,16},{20... | collective-permute-start | bytes 196616 | tf_op jit(solution)/shard_map/ppermute | solution.py:25
  22.1 6.4 %collective-permute-start.2 = (bf16[1,1,256,128]{3,2,1,0:T(8,128)(2,1)S(1)}, bf16[1,1,256,128]{3,2,1,0:T(8,128)(2,1)S(1)}, u32[]{:S(2)}, u32[]{:S(2)}) collective-permute-start(bf16[1,1,256,128]{3,2,1,0:T(8,128)(2,1)S(1)} %collective-permute-done.1), channel_id=1, source_target_pairs={{0,2},{2,4},{4,6},{6,8},{8,10},{10,12},{12,14},{14,16},{16,18},{18... | collective-permute-start | bytes 196616 | tf_op jit(solution)/shard_map/ppermute | solution.py:22
  22.3 11.3 %collective-permute-start.9 = (bf16[1,1,256,128]{3,2,1,0:T(8,128)(2,1)S(1)}, bf16[1,1,256,128]{3,2,1,0:T(8,128)(2,1)S(1)}, u32[]{:S(2)}, u32[]{:S(2)}) collective-permute-start(bf16[1,1,256,128]{3,2,1,0:T(8,128)(2,1)S(1)} %collective-permute-done.8), channel_id=1, source_target_pairs={{2,0},{4,2},{6,4},{8,6},{10,8},{12,10},{14,12},{16,14},{18,16},{20... | collective-permute-start | bytes 196616 | tf_op jit(solution)/shard_map/ppermute | solution.py:25
  28.5 8.8 %collective-permute-start.3 = (bf16[1,1,256,128]{3,2,1,0:T(8,128)(2,1)S(1)}, bf16[1,1,256,128]{3,2,1,0:T(8,128)(2,1)S(1)}, u32[]{:S(2)}, u32[]{:S(2)}) collective-permute-start(bf16[1,1,256,128]{3,2,1,0:T(8,128)(2,1)S(1)} %collective-permute-done.2), channel_id=1, source_target_pairs={{0,2},{2,4},{4,6},{6,8},{8,10},{10,12},{12,14},{14,16},{16,18},{18... | collective-permute-start | bytes 196616 | tf_op jit(solution)/shard_map/ppermute | solution.py:22
  33.6 5.5 %collective-permute-start.10 = (bf16[1,1,256,128]{3,2,1,0:T(8,128)(2,1)S(1)}, bf16[1,1,256,128]{3,2,1,0:T(8,128)(2,1)S(1)}, u32[]{:S(2)}, u32[]{:S(2)}) collective-permute-start(bf16[1,1,256,128]{3,2,1,0:T(8,128)(2,1)S(1)} %collective-permute-done.9), channel_id=1, source_target_pairs={{2,0},{4,2},{6,4},{8,6},{10,8},{12,10},{14,12},{16,14},{18,16},{20... | collective-permute-start | bytes 196616 | tf_op jit(solution)/shard_map/ppermute | solution.py:25
  37.2 6.4 %collective-permute-start.4 = (bf16[1,1,256,128]{3,2,1,0:T(8,128)(2,1)S(1)}, bf16[1,1,256,128]{3,2,1,0:T(8,128)(2,1)S(1)}, u32[]{:S(2)}, u32[]{:S(2)}) collective-permute-start(bf16[1,1,256,128]{3,2,1,0:T(8,128)(2,1)S(1)} %collective-permute-done.3), channel_id=1, source_target_pairs={{0,2},{2,4},{4,6},{6,8},{8,10},{10,12},{12,14},{14,16},{16,18},{18... | collective-permute-start | bytes 196616 | tf_op jit(solution)/shard_map/ppermute | solution.py:22
  39.1 6.4 %collective-permute-start.11 = (bf16[1,1,256,128]{3,2,1,0:T(8,128)(2,1)S(1)}, bf16[1,1,256,128]{3,2,1,0:T(8,128)(2,1)S(1)}, u32[]{:S(2)}, u32[]{:S(2)}) collective-permute-start(bf16[1,1,256,128]{3,2,1,0:T(8,128)(2,1)S(1)} %collective-permute-done.10), channel_id=1, source_target_pairs={{2,0},{4,2},{6,4},{8,6},{10,8},{12,10},{14,12},{16,14},{18,16},{20... | collective-permute-start | bytes 196616 | tf_op jit(solution)/shard_map/ppermute | solution.py:25
  43.6 6.4 %collective-permute-start.5 = (bf16[1,1,256,128]{3,2,1,0:T(8,128)(2,1)S(1)}, bf16[1,1,256,128]{3,2,1,0:T(8,128)(2,1)S(1)}, u32[]{:S(2)}, u32[]{:S(2)}) collective-permute-start(bf16[1,1,256,128]{3,2,1,0:T(8,128)(2,1)S(1)} %collective-permute-done.4), channel_id=1, source_target_pairs={{0,2},{2,4},{4,6},{6,8},{8,10},{10,12},{12,14},{14,16},{16,18},{18... | collective-permute-start | bytes 196616 | tf_op jit(solution)/shard_map/ppermute | solution.py:22
  45.5 6.4 %collective-permute-start.12 = (bf16[1,1,256,128]{3,2,1,0:T(8,128)(2,1)S(1)}, bf16[1,1,256,128]{3,2,1,0:T(8,128)(2,1)S(1)}, u32[]{:S(2)}, u32[]{:S(2)}) collective-permute-start(bf16[1,1,256,128]{3,2,1,0:T(8,128)(2,1)S(1)} %collective-permute-done.11), channel_id=1, source_target_pairs={{2,0},{4,2},{6,4},{8,6},{10,8},{12,10},{14,12},{16,14},{18,16},{20... | collective-permute-start | bytes 196616 | tf_op jit(solution)/shard_map/ppermute | solution.py:25
  50.0 6.4 %collective-permute-start.6 = (bf16[1,1,256,128]{3,2,1,0:T(8,128)(2,1)S(1)}, bf16[1,1,256,128]{3,2,1,0:T(8,128)(2,1)S(1)}, u32[]{:S(2)}, u32[]{:S(2)}) collective-permute-start(bf16[1,1,256,128]{3,2,1,0:T(8,128)(2,1)S(1)} %collective-permute-done.5), channel_id=1, source_target_pairs={{0,2},{2,4},{4,6},{6,8},{8,10},{10,12},{12,14},{14,16},{16,18},{18... | collective-permute-start | bytes 196616 | tf_op jit(solution)/shard_map/ppermute | solution.py:22
  51.9 6.4 %collective-permute-start.13 = (bf16[1,1,256,128]{3,2,1,0:T(8,128)(2,1)S(1)}, bf16[1,1,256,128]{3,2,1,0:T(8,128)(2,1)S(1)}, u32[]{:S(2)}, u32[]{:S(2)}) collective-permute-start(bf16[1,1,256,128]{3,2,1,0:T(8,128)(2,1)S(1)} %collective-permute-done.12), channel_id=1, source_target_pairs={{2,0},{4,2},{6,4},{8,6},{10,8},{12,10},{14,12},{16,14},{18,16},{20... | collective-permute-start | bytes 196616 | tf_op jit(solution)/shard_map/ppermute | solution.py:25
  56.4 6.4 %collective-permute-start.7 = (bf16[1,1,256,128]{3,2,1,0:T(8,128)(2,1)S(1)}, bf16[1,1,256,128]{3,2,1,0:T(8,128)(2,1)S(1)}, u32[]{:S(2)}, u32[]{:S(2)}) collective-permute-start(bf16[1,1,256,128]{3,2,1,0:T(8,128)(2,1)S(1)} %collective-permute-done.6), channel_id=1, source_target_pairs={{0,2},{2,4},{4,6},{6,8},{8,10},{10,12},{12,14},{14,16},{16,18},{18... | collective-permute-start | bytes 196616 | tf_op jit(solution)/shard_map/ppermute | solution.py:22
  58.3 6.4 %collective-permute-start.14 = (bf16[1,1,256,128]{3,2,1,0:T(8,128)(2,1)S(1)}, bf16[1,1,256,128]{3,2,1,0:T(8,128)(2,1)S(1)}, u32[]{:S(2)}, u32[]{:S(2)}) collective-permute-start(bf16[1,1,256,128]{3,2,1,0:T(8,128)(2,1)S(1)} %collective-permute-done.13), channel_id=1, source_target_pairs={{2,0},{4,2},{6,4},{8,6},{10,8},{12,10},{14,12},{16,14},{18,16},{20... | collective-permute-start | bytes 196616 | tf_op jit(solution)/shard_map/ppermute | solution.py:25
  67.4 68.6 %reduce-scatter.2.cloned.1.call-start = ((), (), s32[]{:S(2)}) async-start(), calls=%async_computation.1 | async-start | bytes 2228224 | tf_op jit(solution)/shard_map/reduce_scatter | solution.py:59
  73.4 35.4 %slice-start = ((s8[4718592]{0:T(1024)(128)(4,1)}), s8[524288]{0:T(1024)(128)(4,1)S(1)}, s32[]{:S(2)}) async-start(s8[4718592]{0:T(1024)(128)(4,1)} %bitcast.193), calls=%async_computation.3 | async-start | bytes 1048576
  102.2 1.9 %copy-start = (bf16[1,2,256,2048]{3,2,0,1:T(8,128)(2,1)S(1)}, bf16[1,2,256,2048]{3,2,0,1:T(8,128)(2,1)}, u32[]{:S(2)}) copy-start(bf16[1,2,256,2048]{3,2,0,1:T(8,128)(2,1)} %all-gather.2.cloned.1.call-done) | copy-start | bytes 6291460
  104.1 4.7 %slice-start.1 = ((s8[4718592]{0:T(1024)(128)(4,1)}), s8[4194304]{0:T(1024)(128)(4,1)S(1)}, s32[]{:S(2)}) async-start(s8[4718592]{0:T(1024)(128)(4,1)} %bitcast.193), calls=%async_computation.4 | async-start | bytes 8388608
Sparse Core Ops, SparseCore 0:
  67.6 34.5 all-gather.1
Sparse Core Ops, SparseCore 1:
  73.1 62.9 reduce-scatter.1
